TPU v7x, 32 devices: a whole 2x2x4 slice. The times are simulated.
32 devices in a mesh: fsdp: 8 (over y, x, core), tp: 4 (over z).
Axes of the slice: x: 2, y: 2, z: 4, core: 2. Of those that a mesh axis runs over, the one named last changes fastest.
Arguments:
- roll_rows: bfloat16 [256, 72, 3584], P('fsdp', None, 'tp'), may hold values from -60 to 60
- dest: int32 [256], P('fsdp'), may hold values from 0 to 255, as said below
- lengths: int32 [8, 32], P('fsdp'), may hold values from 1 to 72, 768 in all within a row
- clusters: int32 [256], P('fsdp'), may hold values from 0 to 3
- log_prob_grad: bfloat16 [6144, 3584], P('fsdp', 'tp'), may hold values from -6 to 6
- gain: bfloat16 [3584], replicated, may hold values from 0.5 to 1.5
- w_q: bfloat16 [3584, 2048], P('fsdp', 'tp'), may hold values from -1 to 1
- w_k: bfloat16 [3584, 512], P('fsdp', 'tp'), may hold values from -1 to 1
- w_v: bfloat16 [3584, 512], P('fsdp', 'tp'), may hold values from -0.09375 to 0.09375
- w_o_t: bfloat16 [3584, 2048], P('fsdp', 'tp'), may hold values from -0.125 to 0.125
Outputs:
- input_grad: bfloat16 [6144, 3584], P('fsdp', 'tp')
- grad_q: bfloat16 [3584, 2048], P('fsdp', 'tp')
- grad_k: bfloat16 [3584, 512], P('fsdp', 'tp')
- grad_v: bfloat16 [3584, 512], P('fsdp', 'tp')
- grad_o_t: bfloat16 [3584, 2048], P('fsdp', 'tp')
Inputs may be any that keep to these rules, and one draw needn't show every extreme that they name: dest is a permutation; every rollout replica hands exactly 4 completions to every learner, and every learner trains 32 completions. Each learner's 32 lengths sum to 768.
All inputs are finite; a program needn't handle non-finite values.
Results may differ from a plain program's by a relative error of at most 0.03.
Values may be sent and summed in bfloat16 or wider, within the bound.
No kernel may reach another device: no remote copies, remote signals or barrier semaphores. Data moves between devices by JAX's collectives and lax.ppermute only.
A program may use at most 128 MiB of HBM per device.

v0:
```python
import functools

import jax
import jax.numpy as jnp
from jax import lax
from jax.experimental import pallas as pl
from jax.experimental.pallas import tpu as pltpu
from jax.sharding import PartitionSpec as P

KEY_VALUE_HEADS = 4
HD = 128
QUERY_HEADS = 16
GSIZE = 16
ROPE_BASE = 1000000.0
NORM_EPSILON = 1e-06
BLOCK = 128

UP = [(0, 1), (1, 2), (2, 3)]
DOWN = [(1, 0), (2, 1), (3, 2)]
UP_MID = [(1, 2), (2, 3)]
DOWN_MID = [(1, 0), (2, 1)]
TO_ENDS = [(2, 3), (1, 0)]
FROM_ENDS = [(3, 2), (0, 1)]
UP_IN = [(0, 1), (1, 2)]
DOWN_IN = [(3, 2), (2, 1)]


def contract_rows(left, right):
    return lax.dot_general(
        left, right, (((0,), (0,)), ((), ())), preferred_element_type=jnp.float32
    )


def times_trans(left, right):
    return lax.dot_general(
        left, right, (((1,), (1,)), ((), ())), preferred_element_type=jnp.float32
    )


def matmul(left, right):
    return jnp.dot(left, right, preferred_element_type=jnp.float32)


def gather_near(own):
    return lax.ppermute(own, "tp", UP), lax.ppermute(own, "tp", DOWN)


def gather_far(step1, z):
    up2 = lax.ppermute(step1[0], "tp", UP_MID)
    down2 = lax.ppermute(step1[1], "tp", DOWN_MID)
    return jnp.where(z >= 2, up2, down2)


def gather_end(far2):
    return lax.ppermute(far2, "tp", TO_ENDS)


def shards(own, step1, far2, far3, z):
    up1, down1 = step1
    near = jnp.where(z % 2 == 1, up1, down1)
    other = jnp.where(z == 1, down1, jnp.where(z == 2, up1, far3))
    return [own, near, far2, other]


def after(value, *earlier):
    return lax.optimization_barrier((value, *earlier))[0]


def scatter_end(parts):
    return lax.ppermute(parts[3], "tp", FROM_ENDS)


def scatter_far(parts, from_end):
    total2 = (parts[2].astype(jnp.float32) + from_end.astype(jnp.float32)).astype(jnp.bfloat16)
    return lax.ppermute(total2, "tp", UP_IN), lax.ppermute(total2, "tp", DOWN_IN)


def scatter_near(parts, step2, z):
    own, near, _, other = parts
    f32 = jnp.float32
    up2, down2 = step2
    go_up = jnp.where(z == 1, other, near).astype(f32) + up2.astype(f32)
    go_down = jnp.where(z == 2, other, near).astype(f32) + down2.astype(f32)
    up3 = lax.ppermute(go_up.astype(jnp.bfloat16), "tp", UP)
    down3 = lax.ppermute(go_down.astype(jnp.bfloat16), "tp", DOWN)
    return own.astype(f32) + up3.astype(f32) + down3.astype(f32)


def attention_kernel(has_prev, is_last, first, feature_count, *refs):
    refs = list(refs)
    raw_ref, inv_ref, ga_ref, adv_ref, cos_ref, sin_ref, start_ref = refs[:7]
    refs = refs[7:]
    if has_prev:
        lin_prev, inv_prev, dq_prev, dk_prev, dv_prev = refs[:5]
        refs = refs[5:]
    dqkv_ref, dscaled_ref, mean_ref, out_ref = refs[:4]
    refs = refs[4:]
    if not is_last:
        lin_next, inv_next, dq_next, dk_next, dv_next = refs[:5]
        refs = refs[5:]
    qkv_b, dq_b, dk_acc, dv_acc = refs
    rows = raw_ref.shape[0]
    heads = ga_ref.shape[1] // HD
    qw = heads * HD
    scale = HD ** (-0.5)
    f32, bf16 = jnp.float32, jnp.bfloat16
    blocks = rows // BLOCK

    def span(block):
        return slice(block * BLOCK, (block + 1) * BLOCK)

    def turn(value, cos, sin):
        return value * cos + pltpu.roll(value, HD // 2, 1) * sin

    def whole(block):
        return slice(first + block * BLOCK, first + (block + 1) * BLOCK)

    def linear(block, cols):
        if block < 0:
            return lin_prev[:, cols]
        return raw_ref[span(block), cols] * inv_ref[span(block), :]

    def prepare(block, from_head):
        cos, sin = cos_ref[whole(block), :], sin_ref[whole(block), :]
        for h in range(from_head, heads + 1):
            cols = slice(h * HD, (h + 1) * HD)
            qkv_b[span(block + 1), cols] = turn(linear(block, cols), cos, sin).astype(bf16)
        cols = slice(qw + HD, qw + 2 * HD)
        qkv_b[span(block + 1), cols] = linear(block, cols).astype(bf16)

    if has_prev:
        prepare(-1, heads)
        dq_b[span(0), :] = dq_prev[...]
        dk_acc[span(0), :] = dk_prev[...]
        dv_acc[span(0), :] = dv_prev[...]
    else:
        qkv_b[span(0), :] = jnp.zeros((BLOCK, qkv_b.shape[1]), bf16)
        dk_acc[span(0), :] = jnp.zeros((BLOCK, HD), f32)
        dv_acc[span(0), :] = jnp.zeros((BLOCK, HD), f32)

    for block in range(blocks):
        prepare(block, 0)
        adv = adv_ref[whole(block), :]
        here, after = span(block), span(block + 1)
        both = slice(block * BLOCK, (block + 2) * BLOCK)
        qs = jnp.concatenate(
            [qkv_b[after, h * HD : (h + 1) * HD] for h in range(heads)], axis=0
        )
        gs = jnp.concatenate(
            [(ga_ref[whole(block), h * HD : (h + 1) * HD] * adv).astype(bf16) for h in range(heads)], axis=0
        )
        ks = qkv_b[both, qw : qw + HD]
        vs = qkv_b[both, qw + HD : qw + 2 * HD]
        start = start_ref[whole(block), :] - (first + (block - 1) * BLOCK)
        col = lax.broadcasted_iota(jnp.int32, (BLOCK, 2 * BLOCK), 1)
        row = lax.broadcasted_iota(jnp.int32, (BLOCK, 2 * BLOCK), 0) + BLOCK
        bias = jnp.where((col >= start) & (col <= row), 0.0, -1e30)
        bias = jnp.concatenate([bias] * heads, axis=0)
        scores = times_trans(qs, ks) * scale + bias
        top = jnp.max(scores, axis=-1, keepdims=True)
        weight = jnp.exp(scores - top)
        prob = weight / jnp.sum(weight, axis=-1, keepdims=True)
        prob_b = prob.astype(bf16)
        out = matmul(prob_b, vs)
        grad_prob = times_trans(gs, vs)
        delta = jnp.sum(prob * grad_prob, axis=-1, keepdims=True)
        ds = (prob * (grad_prob - delta) * scale).astype(bf16)
        dq = matmul(ds, ks)
        dk_acc[span(block), :] += contract_rows(ds[:, :BLOCK], qs)
        dk_acc[after, :] = contract_rows(ds[:, BLOCK:], qs)
        dv_acc[span(block), :] += contract_rows(prob_b[:, :BLOCK], gs)
        dv_acc[after, :] = contract_rows(prob_b[:, BLOCK:], gs)
        cos, sin = cos_ref[whole(block), :], sin_ref[whole(block), :]
        for h in range(heads):
            cols = slice(h * HD, (h + 1) * HD)
            out_ref[here, cols] = (out[span(h), :].astype(bf16).astype(f32) * adv).astype(bf16)
            dq_b[after, cols] = turn(dq[span(h), :], cos, -sin).astype(bf16)

    begin = -1 if has_prev else 0
    end = blocks if is_last else blocks - 1
    for block in range(begin, end):
        to = span(block - begin)
        cos, sin = cos_ref[whole(block), :], sin_ref[whole(block), :]
        inv = inv_prev[...] if block < 0 else inv_ref[span(block), :]
        total = jnp.zeros((BLOCK, 1), f32)
        for h in range(heads + 2):
            cols = slice(h * HD, (h + 1) * HD)
            if h < heads:
                grad = dq_b[span(block + 1), cols]
            elif h == heads:
                grad = turn(dk_acc[span(block + 1), :], cos, -sin).astype(bf16)
            else:
                grad = dv_acc[span(block + 1), :].astype(bf16)
            dqkv_ref[to, cols] = grad
            grad = grad.astype(f32)
            dscaled_ref[to, cols] = (grad * inv).astype(bf16)
            total += jnp.sum(grad * linear(block, cols), axis=-1, keepdims=True)
        mean_ref[to, 0:1] = inv
        mean_ref[to, 1:2] = inv * inv * total * (1.0 / feature_count)
    if not is_last:
        inv_next[...] = inv_ref[span(blocks - 1), :]
        lin_next[...] = raw_ref[span(blocks - 1), :] * inv_next[...]
        dq_next[...] = dq_b[span(blocks), :]
        dk_next[...] = dk_acc[span(blocks), :]
        dv_next[...] = dv_acc[span(blocks), :]


def attention(first, total, feature_count, raw, inv, ga, adv, cos, sin, start, prev):
    rows, width = raw.shape
    qw = ga.shape[1]
    is_last = first + rows == total
    final = rows + (BLOCK if prev else 0) - (0 if is_last else BLOCK)
    f32, bf16 = jnp.float32, jnp.bfloat16
    out_shape = [
        jax.ShapeDtypeStruct((final, width), bf16),
        jax.ShapeDtypeStruct((final, width), bf16),
        jax.ShapeDtypeStruct((final, 2), f32),
        jax.ShapeDtypeStruct((rows, qw), bf16),
    ]
    if not is_last:
        out_shape += [
            jax.ShapeDtypeStruct((BLOCK, width), f32),
            jax.ShapeDtypeStruct((BLOCK, 1), f32),
            jax.ShapeDtypeStruct((BLOCK, qw), bf16),
            jax.ShapeDtypeStruct((BLOCK, HD), f32),
            jax.ShapeDtypeStruct((BLOCK, HD), f32),
        ]
    operands = [raw, inv, ga, adv, cos, sin, start] + list(prev)
    vmem = pl.BlockSpec(memory_space=pltpu.VMEM)
    return pl.pallas_call(
        functools.partial(attention_kernel, bool(prev), is_last, first, feature_count),
        out_shape=out_shape,
        in_specs=[vmem] * len(operands),
        out_specs=[vmem] * len(out_shape),
        scratch_shapes=[
            pltpu.VMEM((rows + BLOCK, width), bf16),
            pltpu.VMEM((rows + BLOCK, qw), bf16),
            pltpu.VMEM((rows + BLOCK, HD), f32),
            pltpu.VMEM((rows + BLOCK, HD), f32),
        ],
        compiler_params=pltpu.CompilerParams(vmem_limit_bytes=32 * 1024 * 1024),
        cost_estimate=pl.CostEstimate(
            flops=rows * 2 * BLOCK * HD * 12 * (qw // HD),
            bytes_accessed=rows * width * 8 + rows * qw * 6,
            transcendentals=rows * 2 * BLOCK * (qw // HD),
        ),
        name="attention",
    )(*operands)


def project_kernel(count, feature_count, *refs):
    x_refs, w_refs = refs[:count], refs[count : 2 * count]
    raw_ref, square_ref = refs[-2:]
    raw, squares = None, None
    if len(refs) > 2 * count + 2:
        raw, squares = refs[2 * count][...], refs[2 * count + 1][...]
    for x_ref, w_ref in zip(x_refs, w_refs):
        part = matmul(x_ref[...], w_ref[...])
        raw = part if raw is None else raw + part
        wide = x_ref[...].astype(jnp.float32)
        part = jnp.sum(wide * wide, axis=1, keepdims=True)
        squares = part if squares is None else squares + part
    raw_ref[...] = raw
    if feature_count:
        squares = lax.rsqrt(squares / feature_count + NORM_EPSILON)
    square_ref[...] = squares


def project(parts, weights, prior, feature_count):
    rows, width = parts[0].shape[0], weights[0].shape[1]
    operands = [*parts, *weights, *prior]
    vmem = pl.BlockSpec(memory_space=pltpu.VMEM)
    return pl.pallas_call(
        functools.partial(project_kernel, len(parts), feature_count),
        out_shape=[
            jax.ShapeDtypeStruct((rows, width), jnp.float32),
            jax.ShapeDtypeStruct((rows, 1), jnp.float32),
        ],
        in_specs=[vmem] * len(operands),
        out_specs=[vmem] * 2,
        compiler_params=pltpu.CompilerParams(vmem_limit_bytes=32 * 1024 * 1024),
        cost_estimate=pl.CostEstimate(
            flops=2 * len(parts) * rows * width * parts[0].shape[1],
            bytes_accessed=2 * len(parts) * parts[0].shape[1] * (rows + width) + 8 * rows * width,
            transcendentals=rows,
        ),
        name="project",
    )(*operands)


def weight_grad_kernel(x_count, place_ref, *refs):
    x_refs = refs[: 4 * x_count]
    g_ref, scaled_ref, out_ref, gain_ref, term_ref = refs[4 * x_count :]
    width = scaled_ref.shape[1]
    gain = gain_ref[0]
    gain = jnp.transpose(jnp.broadcast_to(gain, (HD, gain.shape[1])))[:, 0:1]
    term_ref[:, width:] = contract_rows(g_ref[...], out_ref[...]).astype(jnp.bfloat16)
    for k in range(4):

        @pl.when(place_ref[pl.program_id(0)] == k)
        def _():
            total, base = None, 0
            for ref in x_refs[k * x_count : (k + 1) * x_count]:
                part = contract_rows(ref[...], scaled_ref[base : base + ref.shape[0], :])
                base += ref.shape[0]
                total = part if total is None else total + part
            term_ref[:, :width] = (total * gain).astype(jnp.bfloat16)


def weight_grads(places, x_chunks, g_rows, scaled, out, gain):
    features = gain.shape[2]
    width = scaled.shape[1] + out.shape[1]
    x_parts = [chunk[k] for k in range(4) for chunk in x_chunks]

    def once(o):
        return pl.BlockSpec(o.shape, lambda j, place: (0, 0), pipeline_mode=pl.Buffered(1))

    return pl.pallas_call(
        functools.partial(weight_grad_kernel, len(x_chunks)),
        out_shape=jax.ShapeDtypeStruct((4 * features, width), jnp.bfloat16),
        grid_spec=pltpu.PrefetchScalarGridSpec(
            num_scalar_prefetch=1,
            grid=(4,),
            in_specs=[once(x) for x in x_parts]
            + [pl.BlockSpec((g_rows.shape[0], features), lambda j, place: (0, j))]
            + [once(scaled), once(out)]
            + [pl.BlockSpec((1, 1, features), lambda j, place: (j, 0, 0))],
            out_specs=pl.BlockSpec((features, width), lambda j, place: (j, 0)),
        ),
        compiler_params=pltpu.CompilerParams(vmem_limit_bytes=40 * 1024 * 1024),
        cost_estimate=pl.CostEstimate(
            flops=2 * scaled.shape[0] * 4 * features * width,
            bytes_accessed=4 * features * (4 * scaled.shape[0] + 2 * width),
            transcendentals=0,
        ),
        name="weight_grads",
    )(places, *x_parts, g_rows, scaled, out, gain)


def per_device(roll_rows, dest, lengths, clusters, log_prob_grad, gain, w_q, w_k, w_v, w_o_t):
    sequence_count = dest.shape[0]
    max_len, local_features = roll_rows.shape[1:]
    row_count = log_prob_grad.shape[0]
    replicas = lax.axis_size("fsdp")
    per_pair = sequence_count // replicas
    me = lax.axis_index("fsdp")
    z = lax.axis_index("tp")
    f32, bf16 = jnp.float32, jnp.bfloat16
    q_cols, k_cols = w_q.shape[1], w_k.shape[1]
    qkv_cols = q_cols + 2 * k_cols
    feature_count = gain.shape[0]

    g_rows = lax.all_gather(log_prob_grad, "tp", axis=1, tiled=True)

    slot_ids = jnp.arange(sequence_count, dtype=jnp.int32)
    earlier_dest = dest[None, :] < dest[:, None]
    send_block = jnp.sum(earlier_dest.astype(jnp.int32), axis=1)
    source = jnp.sum(
        jnp.where(send_block[None, :] == slot_ids[:, None], slot_ids[None, :], 0), axis=1
    )
    send_rows = jnp.take(roll_rows, source, axis=0, mode="clip")
    arrived_rows = lax.all_to_all(send_rows, "fsdp", split_axis=0, concat_axis=0, tiled=True)

    ballots = clusters.reshape(sequence_count // GSIZE, GSIZE)
    vote_share = jnp.mean((ballots[:, :, None] == ballots[:, None, :]).astype(f32), axis=2)
    advantage = (vote_share - jnp.mean(vote_share, axis=1, keepdims=True)).reshape(sequence_count)
    tags = jnp.stack([(dest % sequence_count).astype(f32), advantage], axis=1)
    picked = send_block[None, :] == slot_ids[:, None]
    tags = jnp.sum(jnp.where(picked[:, :, None], tags[None, :, :], 0.0), axis=1).astype(bf16)
    tags = lax.all_to_all(tags, "fsdp", split_axis=0, concat_axis=0, tiled=True).astype(f32)
    holder = tags[None, :, 0].astype(jnp.int32) == slot_ids[:, None]
    slot_of = jnp.sum(jnp.where(holder, slot_ids[None, :], 0), axis=1)
    seq_advantage = jnp.sum(jnp.where(holder, tags[None, :, 1], 0.0), axis=1)

    lengths_row = lengths.reshape(sequence_count)
    sequence_ends = jnp.cumsum(lengths_row)
    sequence_starts = sequence_ends - lengths_row
    row_index = jnp.arange(row_count, dtype=jnp.int32)
    one_hot = (sequence_ends[None, :] > row_index[:, None]) & (
        sequence_starts[None, :] <= row_index[:, None]
    )
    row_start = jnp.sum(jnp.where(one_hot, sequence_starts[None, :], 0), axis=1)
    position = row_index - row_start
    row_slot = jnp.sum(jnp.where(one_hot, slot_of[None, :], 0), axis=1)
    adv = jnp.sum(jnp.where(one_hot, seq_advantage[None, :], 0.0), axis=1)[:, None]
    half_width = HD // 2
    frequency = ROPE_BASE ** (-(2.0 * jnp.arange(half_width, dtype=f32)) / HD)
    angles = position.astype(f32)[:, None] * frequency[None, :]
    cos, sin = jnp.cos(angles), jnp.sin(angles)
    cos = jnp.concatenate([cos, cos], axis=1)
    sin = jnp.concatenate([-sin, sin], axis=1)

    start = row_start[:, None]
    arrived_rows = after(arrived_rows, cos, sin, start, adv)
    x_own = jnp.take(
        arrived_rows.reshape(sequence_count * max_len, local_features),
        row_slot * max_len + position,
        axis=0,
        mode="clip",
    )
    bounds = [0, row_count - 2 * BLOCK, row_count]
    x_head, x_tail = x_own[: bounds[1], :], x_own[bounds[1] :, :]
    tail_near = gather_near(x_tail)
    head_near = gather_near(after(x_head, tail_near[0]))
    tail_far2 = gather_far((after(tail_near[0], g_rows), tail_near[1]), z)
    head_far2 = gather_far((after(head_near[0], tail_far2), head_near[1]), z)
    tail_end = gather_end(after(tail_far2, *head_near))
    tail_shards = shards(x_tail, tail_near, tail_far2, tail_end, z)

    w_qkv = lax.all_gather(
        jnp.concatenate([w_q, w_k, w_v], axis=1), "fsdp", axis=0, tiled=True
    )
    w_o = lax.all_gather(w_o_t, "fsdp", axis=0, tiled=True)
    gain_f = gain.astype(f32)
    gain_shards = gain_f.reshape(4, 1, local_features)
    w_shards = (w_qkv.astype(f32) * gain_f[:, None]).astype(bf16)
    w_shards = w_shards.reshape(4, local_features, qkv_cols)
    w_k_parts = [lax.dynamic_index_in_dim(w_shards, z ^ k, 0, keepdims=False) for k in range(4)]

    def backward(i, raw, inv, prev):
        return attention(
            bounds[i], row_count, feature_count, raw, inv, ga, adv, cos, sin, start, prev
        )

    def input_terms(dqkv, scales, parts):
        return [
            (
                scales[:, 0:1] * times_trans(dqkv, w_k_parts[k])
                - parts[k].astype(f32) * scales[:, 1:2]
            ).astype(bf16)
            for k in range(4)
        ]

    raw1, inv1 = project(tail_shards, w_k_parts, (), feature_count)
    head_near_shard = jnp.where(z % 2 == 1, head_near[0], head_near[1])
    early = project([x_head, head_near_shard, head_far2], w_k_parts[:3], (), 0)
    head_end = gather_end(after(head_far2, tail_end, raw1, early[0]))
    head_shards = shards(x_head, head_near, head_far2, head_end, z)
    x_chunks = [head_shards, tail_shards]
    ga = matmul(g_rows, after(w_o, early[0]))
    raw0, inv0 = project(head_shards[3:], w_k_parts[3:], early, feature_count)
    dqkv0, scaled0, scales0, out0, *carry = backward(0, raw0, inv0, ())
    final = dqkv0.shape[0]
    terms0 = input_terms(dqkv0, scales0, [x[:final] for x in head_shards])
    end0 = scatter_end(terms0)
    step0 = scatter_far(terms0, end0)
    dx0 = scatter_near(terms0, step0, z)

    dqkv1, scaled1, scales1, out1 = backward(
        1, after(raw1, terms0[3]), inv1, carry
    )
    places = jnp.stack([z ^ j for j in range(4)]).astype(jnp.int32)
    weight_terms = weight_grads(
        places,
        x_chunks,
        g_rows,
        after(jnp.concatenate([scaled0, scaled1], axis=0), end0),
        jnp.concatenate([out0, out1], axis=0),
        gain_shards,
    )
    summed = lax.psum_scatter(weight_terms, "fsdp", scatter_dimension=0, tiled=True)

    terms1 = input_terms(
        after(dqkv1, weight_terms),
        scales1,
        [jnp.concatenate([x[final:], y], axis=0) for x, y in zip(*x_chunks)],
    )
    end1 = scatter_end([*terms1[:3], after(terms1[3], end0)])
    step1 = scatter_far(terms1, after(end1, *step0))
    dx1 = scatter_near(terms1, (after(step1[0], dx0), step1[1]), z)
    dx = jnp.concatenate([dx0, dx1], axis=0)
    input_grad = (adv * log_prob_grad.astype(f32) + dx).astype(bf16)
    grad_q = summed[:, :q_cols]
    grad_k = summed[:, q_cols : q_cols + k_cols]
    grad_v = summed[:, q_cols + k_cols : qkv_cols]
    grad_o_t = summed[:, qkv_cols:]
    return (input_grad, grad_q, grad_k, grad_v, grad_o_t)


def solution(mesh):
    in_specs = (
        P("fsdp", None, "tp"),
        P("fsdp"),
        P("fsdp", None),
        P("fsdp"),
        P("fsdp", "tp"),
        P(),
        P("fsdp", "tp"),
        P("fsdp", "tp"),
        P("fsdp", "tp"),
        P("fsdp", "tp"),
    )
    out_specs = (
        P("fsdp", "tp"),
        P("fsdp", "tp"),
        P("fsdp", "tp"),
        P("fsdp", "tp"),
        P("fsdp", "tp"),
    )
    return jax.shard_map(
        per_device, mesh=mesh, in_specs=in_specs, out_specs=out_specs, check_vma=False
    )
```

profile of v0, /device:TPU:0, one launch (start us, length us, event | category | flops | bytes accessed | tf_op | source)
XLA Modules:
  0.0 367.5 jit_solution(5399570673518045218)
XLA Ops:
  10.7 5.2 %all-to-all-start = ((bf16[8,4,2]{1,2,0:T(2,128)(2,1)}), bf16[8,4,2]{1,2,0:T(2,128)(2,1)S(1)}, u32[]{:S(2)}, u32[]{:S(2)}) async-start(bf16[8,4,2]{1,2,0:T(2,128)(2,1)} %copy.43), calls=%async_computation | async-start | bytes 8192 | tf_op jit(solution)/shard_map/all_to_all | solution.py:370
  16.0 5.2 %gather_fusion = bf16[32,72,896]{2,1,0:T(8,128)(2,1)} fusion(bf16[32,72,896]{2,1,0:T(8,128)(2,1)} %param.10, s32[1024]{0:T(1024)S(1)} %pad_clamp_fusion.1), kind=kCustom, calls=%fused_computation | custom fusion | bytes 8257664 | tf_op jit(solution)/shard_map/jit(_take)/gather | solution.py:361
  21.2 4.7 %all-to-all-start.1 = ((bf16[32,72,896]{2,1,0:T(8,128)(2,1)}), bf16[32,72,896]{2,1,0:T(8,128)(2,1)}, u32[]{:S(2)}, u32[]{:S(2)}) async-start(bf16[32,72,896]{2,1,0:T(8,128)(2,1)} %gather_fusion), calls=%async_computation.1 | async-start | bytes 8257536 | tf_op jit(solution)/shard_map/all_to_all | solution.py:362
  31.8 42.6 %all-to-all-done.1 = bf16[32,72,896]{2,1,0:T(8,128)(2,1)} async-done(((bf16[32,72,896]{2,1,0:T(8,128)(2,1)}), bf16[32,72,896]{2,1,0:T(8,128)(2,1)}, u32[]{:S(2)}, u32[]{:S(2)}) %all-to-all-start.1) | async-done | bytes 4128800 | tf_op jit(solution)/shard_map/all_to_all | solution.py:362
  74.3 6.3 %gather_fusion.1 = bf16[768,896]{1,0:T(8,128)(2,1)S(1)} fusion(bf16[2304,896]{1,0:T(8,128)(2,1)} %bitcast.5, s32[1024]{0:T(1024)S(1)} %pad_clamp_fusion), kind=kCustom, calls=%fused_computation.1 | custom fusion | bytes 2755584 | tf_op jit(solution)/shard_map/jit(_take)/gather | solution.py:395
  86.5 17.1 %collective-permute-done = bf16[256,896]{1,0:T(8,128)(2,1)S(1)} collective-permute-done((bf16[256,896]{1,0:T(8,128)(2,1)S(1)}, bf16[256,896]{1,0:T(8,128)(2,1)S(1)}, u32[]{:S(2)}, u32[]{:S(2)}) %collective-permute-start) | collective-permute-done | bytes 458784 | tf_op jit(solution)/shard_map/ppermute | solution.py:45
  104.9 14.4 %collective-permute-start.2 = (bf16[512,896]{1,0:T(8,128)(2,1)S(1)}, bf16[512,896]{1,0:T(8,128)(2,1)}, u32[]{:S(2)}, u32[]{:S(2)}) collective-permute-start(bf16[512,896]{1,0:T(8,128)(2,1)S(1)} %slice.96.refs_0_), channel_id=1, source_target_pairs={{0,1},{1,2},{2,3},{4,5},{5,6},{6,7},{8,9},{9,10},{10,11},{12,13},{... | collective-permute-start | bytes 2752520 | tf_op jit(solution)/shard_map/ppermute | solution.py:45
  121.0 6.4 %all-gather.4.cloned.1.call-done.refs_8_ = bf16[768,3584]{1,0:T(8,128)(2,1)} async-done(((bf16[768,896]{1,0:T(8,128)(2,1)}), bf16[768,3584]{1,0:T(8,128)(2,1)}) %all-gather.4.cloned.1.call-update) | async-done | bytes 5505040 | tf_op jit(solution)/shard_map/all_gather | solution.py:353
  128.8 22.8 %collective-permute-done.5 = bf16[256,896]{1,0:T(8,128)(2,1)} collective-permute-done((bf16[256,896]{1,0:T(8,128)(2,1)S(1)}, bf16[256,896]{1,0:T(8,128)(2,1)}, u32[]{:S(2)}, u32[]{:S(2)}) %collective-permute-start.5) | collective-permute-done | bytes 458784 | tf_op jit(solution)/shard_map/ppermute | solution.py:50
  159.9 8.3 %collective-permute-done.8 = bf16[256,896]{1,0:T(8,128)(2,1)} collective-permute-done((bf16[256,896]{1,0:T(8,128)(2,1)S(1)}, bf16[256,896]{1,0:T(8,128)(2,1)}, u32[]{:S(2)}, u32[]{:S(2)}) %collective-permute-start.8) | collective-permute-done | bytes 458784 | tf_op jit(solution)/shard_map/ppermute | solution.py:55
  180.1 6.9 %collective-permute-done.7 = bf16[512,896]{1,0:T(8,128)(2,1)} collective-permute-done((bf16[512,896]{1,0:T(8,128)(2,1)}, bf16[512,896]{1,0:T(8,128)(2,1)}, u32[]{:S(2)}, u32[]{:S(2)}) %collective-permute-start.7) | collective-permute-done | bytes 917536 | tf_op jit(solution)/shard_map/ppermute | solution.py:50
  197.8 10.5 %all-gather.8.cloned.1.call-done = bf16[3584,512]{1,0:T(8,128)(2,1)} async-done(((bf16[448,512]{1,0:T(8,128)(2,1)}), bf16[3584,512]{1,0:T(8,128)(2,1)}) %all-gather.8.cloned.1.call-update) | async-done | bytes 3670032 | tf_op jit(solution)/shard_map/all_gather | solution.py:413
  208.3 6.1 %convolution_bitcast_fusion.refs_2_ = f32[768,512]{1,0:T(8,128)S(1)} fusion(bf16[768,3584]{1,0:T(8,128)(2,1)} %all-gather.4.cloned.1.call-done.refs_8_, bf16[3584,512]{1,0:T(8,128)(2,1)} %all-gather.8.cloned.1.call-done), kind=kOutput, calls=%fused_computation.5 | convolution fusion | flops 2818572288 | bytes 10747904 | tf_op jit(solution)/shard_map/dot_general | solution.py:41
  221.1 8.8 %attention.2 = (bf16[384,768]{1,0:T(8,128)(2,1)S(1)}, bf16[384,768]{1,0:T(8,128)(2,1)S(1)}, f32[384,2]{1,0:T(8,128)S(1)}, bf16[512,512]{1,0:T(8,128)(2,1)S(1)}, ...) custom-call(f32[512,768]{1,0:T(8,128)S(1)} %get-tuple-element.46.ref, ...), custom_call_target="tpu_custom_call" | custom-call | flops 805306368 | bytes 4718592 | tf_op jit(solution)/shard_map/attention/pallas_call | solution.py:230
  245.9 5.6 %attention.3 = (bf16[384,768]{1,0:T(8,128)(2,1)S(1)}, bf16[384,768]{1,0:T(8,128)(2,1)S(1)}, f32[384,2]{1,0:T(8,128)S(1)}, bf16[256,512]{1,0:T(8,128)(2,1)S(1)}) custom-call(f32[256,768]{1,0:T(8,128)S(1)} %copy-done.34, f32[256,1]{1,0:T(8,128)S(1)} %copy-done.44, f32[768,512]{1,0:T(8,128)S(1)} %copy-done.1, f32[768,1]{1,0:T(8,128)S(1)} %copy-done.11, ...), custom_call_target="tpu_custom_call" | custom-call | flops 402653184 | bytes 2359296 | tf_op jit(solution)/shard_map/attention/pallas_call | solution.py:230
  256.4 12.5 %weight_grads.1 = bf16[3584,1280]{1,0:T(8,128)(2,1)} custom-call(s32[4]{0:T(128)S(1)} %pad_add_fusion.place_ref, bf16[512,896]{1,0:T(8,128)(2,1)S(1)} %copy-done.32, bf16[256,896]{1,0:T(8,128)(2,1)S(1)} %copy-done.24, bf16[512,896]{1,0:T(8,128)(2,1)S(1)} %copy-done.28, bf16[256,896]{1,0:T(8,128)(2,1)S(1)} %copy-done.17, ...), custom_call_target="tpu_custom_call" | custom-call | flops 7046430720 | bytes 20185088 | tf_op jit(solution)/shard_map/weight_grads/pallas_call | solution.py:318
  278.7 10.8 %collective-permute-done.11 = bf16[384,896]{1,0:T(8,128)(2,1)S(1)} collective-permute-done((bf16[384,896]{1,0:T(8,128)(2,1)S(1)}, bf16[384,896]{1,0:T(8,128)(2,1)S(1)}, u32[]{:S(2)}, u32[]{:S(2)}) %collective-permute-start.11) | collective-permute-done | bytes 688160 | tf_op jit(solution)/shard_map/ppermute | solution.py:75
  291.7 4.4 %collective-permute-start.12 = (bf16[384,896]{1,0:T(8,128)(2,1)S(1)}, bf16[384,896]{1,0:T(8,128)(2,1)S(1)}, u32[]{:S(2)}, u32[]{:S(2)}) collective-permute-start(bf16[384,896]{1,0:T(8,128)(2,1)S(1)} %get-tuple-element.81), channel_id=1, source_target_pairs={{0,1},{1,2},{2,3},{4,5},{5,6},{6,7},{8,9},{9,10},{10,11},{12,13},{... | collective-permute-start | bytes 2064392 | tf_op jit(solution)/shard_map/ppermute | solution.py:84
  297.7 6.5 %collective-permute-done.15 = bf16[384,896]{1,0:T(8,128)(2,1)S(1)} collective-permute-done((bf16[384,896]{1,0:T(8,128)(2,1)S(1)}, bf16[384,896]{1,0:T(8,128)(2,1)S(1)}, u32[]{:S(2)}, u32[]{:S(2)}) %collective-permute-start.15) | collective-permute-done | bytes 688160 | tf_op jit(solution)/shard_map/ppermute | solution.py:70
  304.6 4.6 %collective-permute-start.16 = (bf16[384,896]{1,0:T(8,128)(2,1)S(1)}, bf16[384,896]{1,0:T(8,128)(2,1)S(1)}, u32[]{:S(2)}, u32[]{:S(2)}) collective-permute-start(bf16[384,896]{1,0:T(8,128)(2,1)S(1)} %add_convert_fusion.2), channel_id=1, source_target_pairs={{0,1},{1,2},{4,5},{5,6},{8,9},{9,10},{12,13},{13,14},{16,17},{17,1... | collective-permute-start | bytes 2064392 | tf_op jit(solution)/shard_map/ppermute | solution.py:75
  311.6 7.4 %collective-permute-done.12 = bf16[384,896]{1,0:T(8,128)(2,1)S(1)} collective-permute-done((bf16[384,896]{1,0:T(8,128)(2,1)S(1)}, bf16[384,896]{1,0:T(8,128)(2,1)S(1)}, u32[]{:S(2)}, u32[]{:S(2)}) %collective-permute-start.12) | collective-permute-done | bytes 688160 | tf_op jit(solution)/shard_map/ppermute | solution.py:84
  319.2 12.5 %collective-permute-done.16 = bf16[384,896]{1,0:T(8,128)(2,1)S(1)} collective-permute-done((bf16[384,896]{1,0:T(8,128)(2,1)S(1)}, bf16[384,896]{1,0:T(8,128)(2,1)S(1)}, u32[]{:S(2)}, u32[]{:S(2)}) %collective-permute-start.16) | collective-permute-done | bytes 688160 | tf_op jit(solution)/shard_map/ppermute | solution.py:75
  338.8 10.9 %collective-permute-done.17 = bf16[384,896]{1,0:T(8,128)(2,1)S(1)} collective-permute-done((bf16[384,896]{1,0:T(8,128)(2,1)S(1)}, bf16[384,896]{1,0:T(8,128)(2,1)S(1)}, u32[]{:S(2)}, u32[]{:S(2)}) %collective-permute-start.17) | collective-permute-done | bytes 688160 | tf_op jit(solution)/shard_map/ppermute | solution.py:84
  349.6 5.5 %collective-permute-done.19 = bf16[384,896]{1,0:T(8,128)(2,1)S(1)} collective-permute-done((bf16[384,896]{1,0:T(8,128)(2,1)S(1)}, bf16[384,896]{1,0:T(8,128)(2,1)S(1)}, u32[]{:S(2)}, u32[]{:S(2)}) %collective-permute-start.19) | collective-permute-done | bytes 688160 | tf_op jit(solution)/shard_map/ppermute | solution.py:85
  (266 shorter events, 106.5 us)
Async XLA Ops:
  7.2 120.2 %all-gather.4.cloned.1.call-start = ((), (), s32[]{:S(2)}) async-start(), calls=%async_computation.3 | async-start | bytes 6881280 | tf_op jit(solution)/shard_map/all_gather | solution.py:353
  8.0 163.9 %all-gather.6.cloned.1.call-start = ((), (), s32[]{:S(2)}) async-start(), calls=%async_computation.4 | async-start | bytes 6193152 | tf_op jit(solution)/shard_map/all_gather | solution.py:410
  21.2 53.1 %all-to-all-start.1 = ((bf16[32,72,896]{2,1,0:T(8,128)(2,1)}), bf16[32,72,896]{2,1,0:T(8,128)(2,1)}, u32[]{:S(2)}, u32[]{:S(2)}) async-start(bf16[32,72,896]{2,1,0:T(8,128)(2,1)} %gather_fusion), calls=%async_computation.1 | async-start | bytes 8257536 | tf_op jit(solution)/shard_map/all_to_all | solution.py:362
  25.9 182.4 %all-gather.8.cloned.1.call-start = ((), (), s32[]{:S(2)}) async-start(), calls=%async_computation.5 | async-start | bytes 4128768 | tf_op jit(solution)/shard_map/all_gather | solution.py:413
  26.7 330.3 %reduce-scatter.2.cloned.1.call-start = ((), (), s32[]{:S(2)}) async-start(), calls=%async_computation.6 | async-start | bytes 10321920 | tf_op jit(solution)/shard_map/reduce_scatter | solution.py:461
  80.7 22.9 %collective-permute-start = (bf16[256,896]{1,0:T(8,128)(2,1)S(1)}, bf16[256,896]{1,0:T(8,128)(2,1)S(1)}, u32[]{:S(2)}, u32[]{:S(2)}) collective-permute-start(bf16[256,896]{1,0:T(8,128)(2,1)S(1)} %slice.97.refs_0_.refs_1_), channel_id=1, source_target_pairs={{0,1},{1,2},{2,3},{4,5},{5,6},{6,7},{8,9},{9,10},{10,11},{12,13},{... | collective-permute-start | bytes 1376264 | tf_op jit(solution)/shard_map/ppermute | solution.py:45
  84.3 35.4 %collective-permute-start.4 = (bf16[256,896]{1,0:T(8,128)(2,1)S(1)}, bf16[256,896]{1,0:T(8,128)(2,1)S(1)}, u32[]{:S(2)}, u32[]{:S(2)}) collective-permute-start(bf16[256,896]{1,0:T(8,128)(2,1)S(1)} %slice.97.refs_0_.refs_1_), channel_id=1, source_target_pairs={{1,0},{2,1},{3,2},{5,4},{6,5},{7,6},{9,8},{10,9},{11,10},{13,12},{... | collective-permute-start | bytes 1376264 | tf_op jit(solution)/shard_map/ppermute | solution.py:45
  103.6 49.1 %collective-permute-start.1 = (bf16[512,896]{1,0:T(8,128)(2,1)S(1)}, bf16[512,896]{1,0:T(8,128)(2,1)}, u32[]{:S(2)}, u32[]{:S(2)}) collective-permute-start(bf16[512,896]{1,0:T(8,128)(2,1)S(1)} %slice.96.refs_0_), channel_id=1, source_target_pairs={{1,0},{2,1},{3,2},{5,4},{6,5},{7,6},{9,8},{10,9},{11,10},{13,12},{... | collective-permute-start | bytes 2752520 | tf_op jit(solution)/shard_map/ppermute | solution.py:45
  104.9 47.8 %collective-permute-start.2 = (bf16[512,896]{1,0:T(8,128)(2,1)S(1)}, bf16[512,896]{1,0:T(8,128)(2,1)}, u32[]{:S(2)}, u32[]{:S(2)}) collective-permute-start(bf16[512,896]{1,0:T(8,128)(2,1)S(1)} %slice.96.refs_0_), channel_id=1, source_target_pairs={{0,1},{1,2},{2,3},{4,5},{5,6},{6,7},{8,9},{9,10},{10,11},{12,13},{... | collective-permute-start | bytes 2752520 | tf_op jit(solution)/shard_map/ppermute | solution.py:45
  119.7 31.9 %collective-permute-start.5 = (bf16[256,896]{1,0:T(8,128)(2,1)S(1)}, bf16[256,896]{1,0:T(8,128)(2,1)}, u32[]{:S(2)}, u32[]{:S(2)}) collective-permute-start(bf16[256,896]{1,0:T(8,128)(2,1)S(1)} %collective-permute-done.4), channel_id=1, source_target_pairs={{1,0},{2,1},{5,4},{6,5},{9,8},{10,9},{13,12},{14,13},{17,16},{18,1... | collective-permute-start | bytes 1376264 | tf_op jit(solution)/shard_map/ppermute | solution.py:50
  127.4 24.2 %collective-permute-start.3 = (bf16[256,896]{1,0:T(8,128)(2,1)S(1)}, bf16[256,896]{1,0:T(8,128)(2,1)}, u32[]{:S(2)}, u32[]{:S(2)}) collective-permute-start(bf16[256,896]{1,0:T(8,128)(2,1)S(1)} %collective-permute-done), channel_id=1, source_target_pairs={{1,2},{2,3},{5,6},{6,7},{9,10},{10,11},{13,14},{14,15},{17,18},{18... | collective-permute-start | bytes 1376264 | tf_op jit(solution)/shard_map/ppermute | solution.py:49
  154.1 32.9 %collective-permute-start.7 = (bf16[512,896]{1,0:T(8,128)(2,1)}, bf16[512,896]{1,0:T(8,128)(2,1)}, u32[]{:S(2)}, u32[]{:S(2)}) collective-permute-start(bf16[512,896]{1,0:T(8,128)(2,1)} %collective-permute-done.1), channel_id=1, source_target_pairs={{1,0},{2,1},{5,4},{6,5},{9,8},{10,9},{13,12},{14,13},{17,16},{18,1... | collective-permute-start | bytes 2752520 | tf_op jit(solution)/shard_map/ppermute | solution.py:50
  157.8 29.3 %collective-permute-start.6 = (bf16[512,896]{1,0:T(8,128)(2,1)}, bf16[512,896]{1,0:T(8,128)(2,1)}, u32[]{:S(2)}, u32[]{:S(2)}) collective-permute-start(bf16[512,896]{1,0:T(8,128)(2,1)} %collective-permute-done.2), channel_id=1, source_target_pairs={{1,2},{2,3},{5,6},{6,7},{9,10},{10,11},{13,14},{14,15},{17,18},{18... | collective-permute-start | bytes 2752520 | tf_op jit(solution)/shard_map/ppermute | solution.py:49
  194.4 23.7 %collective-permute-start.9 = (bf16[512,896]{1,0:T(8,128)(2,1)}, bf16[512,896]{1,0:T(8,128)(2,1)}, u32[]{:S(2)}, u32[]{:S(2)}) collective-permute-start(bf16[512,896]{1,0:T(8,128)(2,1)} %broadcast_select_fusion.1.refs_2_.refs_4_), channel_id=1, source_target_pairs={{2,3},{1,0},{6,7},{5,4},{10,11},{9,8},{14,15},{13,12},{18,19},{17,... | collective-permute-start | bytes 2752520 | tf_op jit(solution)/shard_map/ppermute | solution.py:55
  232.1 20.9 %collective-permute-start.10 = (bf16[384,896]{1,0:T(8,128)(2,1)}, bf16[384,896]{1,0:T(8,128)(2,1)}, u32[]{:S(2)}, u32[]{:S(2)}) collective-permute-start(bf16[384,896]{1,0:T(8,128)(2,1)} %subtract_convert_fusion.5), channel_id=1, source_target_pairs={{3,2},{0,1},{7,6},{4,5},{11,10},{8,9},{15,14},{12,13},{19,18},{16,... | collective-permute-start | bytes 2064392 | tf_op jit(solution)/shard_map/ppermute | solution.py:70
  272.3 17.2 %collective-permute-start.11 = (bf16[384,896]{1,0:T(8,128)(2,1)S(1)}, bf16[384,896]{1,0:T(8,128)(2,1)S(1)}, u32[]{:S(2)}, u32[]{:S(2)}) collective-permute-start(bf16[384,896]{1,0:T(8,128)(2,1)S(1)} %add_convert_fusion.5), channel_id=1, source_target_pairs={{0,1},{1,2},{4,5},{5,6},{8,9},{9,10},{12,13},{13,14},{16,17},{17,1... | collective-permute-start | bytes 2064392 | tf_op jit(solution)/shard_map/ppermute | solution.py:75
  273.7 15.8 %collective-permute-start.13 = (bf16[384,896]{1,0:T(8,128)(2,1)S(1)}, bf16[384,896]{1,0:T(8,128)(2,1)S(1)}, u32[]{:S(2)}, u32[]{:S(2)}) collective-permute-start(bf16[384,896]{1,0:T(8,128)(2,1)S(1)} %add_convert_fusion.5), channel_id=1, source_target_pairs={{3,2},{2,1},{7,6},{6,5},{11,10},{10,9},{15,14},{14,13},{19,18},{18... | collective-permute-start | bytes 2064392 | tf_op jit(solution)/shard_map/ppermute | solution.py:75
  275.5 28.7 %collective-permute-start.15 = (bf16[384,896]{1,0:T(8,128)(2,1)S(1)}, bf16[384,896]{1,0:T(8,128)(2,1)S(1)}, u32[]{:S(2)}, u32[]{:S(2)}) collective-permute-start(bf16[384,896]{1,0:T(8,128)(2,1)S(1)} %subtract_convert_fusion.2), channel_id=1, source_target_pairs={{3,2},{0,1},{7,6},{4,5},{11,10},{8,9},{15,14},{12,13},{19,18},{16,... | collective-permute-start | bytes 2064392 | tf_op jit(solution)/shard_map/ppermute | solution.py:70
  291.7 27.3 %collective-permute-start.12 = (bf16[384,896]{1,0:T(8,128)(2,1)S(1)}, bf16[384,896]{1,0:T(8,128)(2,1)S(1)}, u32[]{:S(2)}, u32[]{:S(2)}) collective-permute-start(bf16[384,896]{1,0:T(8,128)(2,1)S(1)} %get-tuple-element.81), channel_id=1, source_target_pairs={{0,1},{1,2},{2,3},{4,5},{5,6},{6,7},{8,9},{9,10},{10,11},{12,13},{... | collective-permute-start | bytes 2064392 | tf_op jit(solution)/shard_map/ppermute | solution.py:84
  296.2 22.8 %collective-permute-start.14 = (bf16[384,896]{1,0:T(8,128)(2,1)S(1)}, bf16[384,896]{1,0:T(8,128)(2,1)S(1)}, u32[]{:S(2)}, u32[]{:S(2)}) collective-permute-start(bf16[384,896]{1,0:T(8,128)(2,1)S(1)} %get-tuple-element.82), channel_id=1, source_target_pairs={{1,0},{2,1},{3,2},{5,4},{6,5},{7,6},{9,8},{10,9},{11,10},{13,12},{... | collective-permute-start | bytes 2064392 | tf_op jit(solution)/shard_map/ppermute | solution.py:85
  304.6 27.1 %collective-permute-start.16 = (bf16[384,896]{1,0:T(8,128)(2,1)S(1)}, bf16[384,896]{1,0:T(8,128)(2,1)S(1)}, u32[]{:S(2)}, u32[]{:S(2)}) collective-permute-start(bf16[384,896]{1,0:T(8,128)(2,1)S(1)} %add_convert_fusion.2), channel_id=1, source_target_pairs={{0,1},{1,2},{4,5},{5,6},{8,9},{9,10},{12,13},{13,14},{16,17},{17,1... | collective-permute-start | bytes 2064392 | tf_op jit(solution)/shard_map/ppermute | solution.py:75
  309.2 22.6 %collective-permute-start.18 = (bf16[384,896]{1,0:T(8,128)(2,1)S(1)}, bf16[384,896]{1,0:T(8,128)(2,1)S(1)}, u32[]{:S(2)}, u32[]{:S(2)}) collective-permute-start(bf16[384,896]{1,0:T(8,128)(2,1)S(1)} %add_convert_fusion.2), channel_id=1, source_target_pairs={{3,2},{2,1},{7,6},{6,5},{11,10},{10,9},{15,14},{14,13},{19,18},{18... | collective-permute-start | bytes 2064392 | tf_op jit(solution)/shard_map/ppermute | solution.py:75
  332.2 17.5 %collective-permute-start.17 = (bf16[384,896]{1,0:T(8,128)(2,1)S(1)}, bf16[384,896]{1,0:T(8,128)(2,1)S(1)}, u32[]{:S(2)}, u32[]{:S(2)}) collective-permute-start(bf16[384,896]{1,0:T(8,128)(2,1)S(1)} %get-tuple-element.79), channel_id=1, source_target_pairs={{0,1},{1,2},{2,3},{4,5},{5,6},{6,7},{8,9},{9,10},{10,11},{12,13},{... | collective-permute-start | bytes 2064392 | tf_op jit(solution)/shard_map/ppermute | solution.py:84
  336.6 18.5 %collective-permute-start.19 = (bf16[384,896]{1,0:T(8,128)(2,1)S(1)}, bf16[384,896]{1,0:T(8,128)(2,1)S(1)}, u32[]{:S(2)}, u32[]{:S(2)}) collective-permute-start(bf16[384,896]{1,0:T(8,128)(2,1)S(1)} %get-tuple-element.80), channel_id=1, source_target_pairs={{1,0},{2,1},{3,2},{5,4},{6,5},{7,6},{9,8},{10,9},{11,10},{13,12},{... | collective-permute-start | bytes 2064392 | tf_op jit(solution)/shard_map/ppermute | solution.py:85
  (79 other events, 584.9 us)
Sparse Core Ops, SparseCore 0:
  9.6 117.7 all-gather.3
  129.8 41.9 all-gather.5
  173.7 34.5 all-gather.7
  269.0 74.4 reduce-scatter.1
where the time goes:
time: 374 us; the launch traced here: 368 us
  waiting for transfers between devices  175 us (47%)
  starting transfers between devices  63.7 us (17%)
  local copies, waits for them, and re-layouts  42.2 us (11%)
  Pallas kernels  33.6 us (9%)
  other arithmetic  21.1 us (6%)
  matrix products  16.3 us (4%)
  between operations  15.2 us (4%)
    all_to_all x1, waiting for transfers between devices, per_device(): lax.all_to_all(send_rows, 'fsdp', split_axis=0, concat_axis=0, tiled=True)  42.6 us
    ppermute x2, waiting for transfers between devices, gather_far(): down2 = lax.ppermute(step1[1], 'tp', DOWN_MID)  29.7 us
    ppermute x2, waiting for transfers between devices, scatter_far(): lax.ppermute(total2, 'tp', UP_IN)  23.4 us
    unnamed x150, local copies, waits for them, and re-layouts  21.8 us
    ppermute x4, starting transfers between devices, gather_near(): return (lax.ppermute(own, 'tp', UP), lax.ppermute(own, 'tp', DOWN))  20.6 us
    ppermute x2, waiting for transfers between devices, scatter_near(): up3 = lax.ppermute(go_up.astype(jnp.bfloat16), 'tp', UP)  18.3 us
    ppermute x4, waiting for transfers between devices, gather_near(): return (lax.ppermute(own, 'tp', UP), lax.ppermute(own, 'tp', DOWN))  17.5 us
    pallas_call x2, Pallas kernels, attention(): pl.pallas_call(functools.partial(attention_kernel, bool(prev), is_last, f...  14.4 us
  transfers between devices with their start and end apart: 26, of which 16 were waited for; matrix products, arithmetic and copies ran while one was open for 14% of the time, Pallas kernels for 3%

commit v1 on v0

--- a/solution.py
+++ b/solution.py
@@ -70,8 +70,11 @@
     return lax.ppermute(parts[3], "tp", FROM_ENDS)
 
 
-def scatter_far(parts, from_end):
-    total2 = (parts[2].astype(jnp.float32) + from_end.astype(jnp.float32)).astype(jnp.bfloat16)
+def far_total(parts, from_end):
+    return (parts[2].astype(jnp.float32) + from_end.astype(jnp.float32)).astype(jnp.bfloat16)
+
+
+def scatter_far(total2):
     return lax.ppermute(total2, "tp", UP_IN), lax.ppermute(total2, "tp", DOWN_IN)
 
 
@@ -147,7 +150,7 @@
             [qkv_b[after, h * HD : (h + 1) * HD] for h in range(heads)], axis=0
         )
         gs = jnp.concatenate(
-            [(ga_ref[whole(block), h * HD : (h + 1) * HD] * adv).astype(bf16) for h in range(heads)], axis=0
+            [(ga_ref[here, h * HD : (h + 1) * HD] * adv).astype(bf16) for h in range(heads)], axis=0
         )
         ks = qkv_b[both, qw : qw + HD]
         vs = qkv_b[both, qw + HD : qw + 2 * HD]
@@ -288,42 +291,38 @@
     )(*operands)
 
 
-def weight_grad_kernel(x_count, place_ref, *refs):
-    x_refs = refs[: 4 * x_count]
-    g_ref, scaled_ref, out_ref, gain_ref, term_ref = refs[4 * x_count :]
+def weight_grad_kernel(place_ref, *refs):
+    heads, tails, g_tails = refs[:4], refs[4:8], refs[8:12]
+    g_ref, scaled_ref, out_ref, gain_ref, term_ref = refs[12:]
     width = scaled_ref.shape[1]
     gain = gain_ref[0]
     gain = jnp.transpose(jnp.broadcast_to(gain, (HD, gain.shape[1])))[:, 0:1]
-    term_ref[:, width:] = contract_rows(g_ref[...], out_ref[...]).astype(jnp.bfloat16)
+    first = g_ref.shape[0]
     for k in range(4):
 
         @pl.when(place_ref[pl.program_id(0)] == k)
         def _():
-            total, base = None, 0
-            for ref in x_refs[k * x_count : (k + 1) * x_count]:
-                part = contract_rows(ref[...], scaled_ref[base : base + ref.shape[0], :])
-                base += ref.shape[0]
-                total = part if total is None else total + part
+            total = contract_rows(heads[k][...], scaled_ref[:first, :])
+            total += contract_rows(tails[k][...], scaled_ref[first:, :])
             term_ref[:, :width] = (total * gain).astype(jnp.bfloat16)
-
-
-def weight_grads(places, x_chunks, g_rows, scaled, out, gain):
+            total = contract_rows(g_ref[...], out_ref[:first, :])
+            total += contract_rows(g_tails[k][...], out_ref[first:, :])
+            term_ref[:, width:] = total.astype(jnp.bfloat16)
+
+
+def weight_grads(places, heads, tails, g_tails, g_rows, scaled, out, gain):
     features = gain.shape[2]
     width = scaled.shape[1] + out.shape[1]
-    x_parts = [chunk[k] for k in range(4) for chunk in x_chunks]
-
-    def once(o):
-        return pl.BlockSpec(o.shape, lambda j, place: (0, 0), pipeline_mode=pl.Buffered(1))
-
+    vmem = pl.BlockSpec(memory_space=pltpu.VMEM)
     return pl.pallas_call(
-        functools.partial(weight_grad_kernel, len(x_chunks)),
+        weight_grad_kernel,
         out_shape=jax.ShapeDtypeStruct((4 * features, width), jnp.bfloat16),
         grid_spec=pltpu.PrefetchScalarGridSpec(
             num_scalar_prefetch=1,
             grid=(4,),
-            in_specs=[once(x) for x in x_parts]
+            in_specs=[vmem] * 12
             + [pl.BlockSpec((g_rows.shape[0], features), lambda j, place: (0, j))]
-            + [once(scaled), once(out)]
+            + [vmem] * 2
             + [pl.BlockSpec((1, 1, features), lambda j, place: (j, 0, 0))],
             out_specs=pl.BlockSpec((features, width), lambda j, place: (j, 0)),
         ),
@@ -334,7 +333,7 @@
             transcendentals=0,
         ),
         name="weight_grads",
-    )(places, *x_parts, g_rows, scaled, out, gain)
+    )(places, *heads, *tails, *g_tails, g_rows, scaled, out, gain)
 
 
 def per_device(roll_rows, dest, lengths, clusters, log_prob_grad, gain, w_q, w_k, w_v, w_o_t):
@@ -350,7 +349,13 @@
     qkv_cols = q_cols + 2 * k_cols
     feature_count = gain.shape[0]
 
-    g_rows = lax.all_gather(log_prob_grad, "tp", axis=1, tiled=True)
+    bounds = [0, row_count - 2 * BLOCK, row_count]
+    g_rows = lax.all_gather(log_prob_grad[: bounds[1], :], "tp", axis=1, tiled=True)
+    g_tail = log_prob_grad[bounds[1] :, :]
+    g_near = gather_near(g_tail)
+    g_far2 = gather_far(g_near, z)
+    g_end = gather_end(g_far2)
+    g_shards = shards(g_tail, g_near, g_far2, g_end, z)
 
     slot_ids = jnp.arange(sequence_count, dtype=jnp.int32)
     earlier_dest = dest[None, :] < dest[:, None]
@@ -391,17 +396,16 @@
     sin = jnp.concatenate([-sin, sin], axis=1)
 
     start = row_start[:, None]
-    arrived_rows = after(arrived_rows, cos, sin, start, adv)
+    arrived_rows = after(arrived_rows, cos, sin, start, adv, g_far2)
     x_own = jnp.take(
         arrived_rows.reshape(sequence_count * max_len, local_features),
         row_slot * max_len + position,
         axis=0,
         mode="clip",
     )
-    bounds = [0, row_count - 2 * BLOCK, row_count]
     x_head, x_tail = x_own[: bounds[1], :], x_own[bounds[1] :, :]
     tail_near = gather_near(x_tail)
-    head_near = gather_near(after(x_head, tail_near[0]))
+    head_near = gather_near(after(x_head, tail_near[0], g_end))
     tail_far2 = gather_far((after(tail_near[0], g_rows), tail_near[1]), z)
     head_far2 = gather_far((after(head_near[0], tail_far2), head_near[1]), z)
     tail_end = gather_end(after(tail_far2, *head_near))
@@ -419,7 +423,7 @@
 
     def backward(i, raw, inv, prev):
         return attention(
-            bounds[i], row_count, feature_count, raw, inv, ga, adv, cos, sin, start, prev
+            bounds[i], row_count, feature_count, raw, inv, ga[i], adv, cos, sin, start, prev
         )
 
     def input_terms(dqkv, scales, parts):
@@ -437,13 +441,22 @@
     head_end = gather_end(after(head_far2, tail_end, raw1, early[0]))
     head_shards = shards(x_head, head_near, head_far2, head_end, z)
     x_chunks = [head_shards, tail_shards]
-    ga = matmul(g_rows, after(w_o, early[0]))
+    w_o = after(w_o, early[0])
+    o_shards = w_o.reshape(4, local_features, q_cols)
+    ga = [
+        matmul(g_rows, w_o),
+        sum(
+            matmul(g_shards[k], lax.dynamic_index_in_dim(o_shards, z ^ k, 0, keepdims=False))
+            for k in range(4)
+        ),
+    ]
     raw0, inv0 = project(head_shards[3:], w_k_parts[3:], early, feature_count)
     dqkv0, scaled0, scales0, out0, *carry = backward(0, raw0, inv0, ())
     final = dqkv0.shape[0]
     terms0 = input_terms(dqkv0, scales0, [x[:final] for x in head_shards])
     end0 = scatter_end(terms0)
-    step0 = scatter_far(terms0, end0)
+    total0 = far_total(terms0, end0)
+    step0 = scatter_far(total0)
     dx0 = scatter_near(terms0, step0, z)
 
     dqkv1, scaled1, scales1, out1 = backward(
@@ -452,9 +465,11 @@
     places = jnp.stack([z ^ j for j in range(4)]).astype(jnp.int32)
     weight_terms = weight_grads(
         places,
-        x_chunks,
+        head_shards,
+        tail_shards,
+        g_shards,
         g_rows,
-        after(jnp.concatenate([scaled0, scaled1], axis=0), end0),
+        after(jnp.concatenate([scaled0, scaled1], axis=0), total0),
         jnp.concatenate([out0, out1], axis=0),
         gain_shards,
     )
@@ -466,7 +481,7 @@
         [jnp.concatenate([x[final:], y], axis=0) for x, y in zip(*x_chunks)],
     )
     end1 = scatter_end([*terms1[:3], after(terms1[3], end0)])
-    step1 = scatter_far(terms1, after(end1, *step0))
+    step1 = scatter_far(far_total(terms1, after(end1, *step0)))
     dx1 = scatter_near(terms1, (after(step1[0], dx0), step1[1]), z)
     dx = jnp.concatenate([dx0, dx1], axis=0)
     input_grad = (adv * log_prob_grad.astype(f32) + dx).astype(bf16)

time: 374 us -> 380 us (1.016)
  starting transfers between devices: 63.7 us -> 89.4 us
  waiting for transfers between devices: 175 us -> 169 us
  local copies, waits for them, and re-layouts: 42.2 us -> 37.1 us
    all_to_all x1, waiting for transfers between devices: 42.6 us -> 0.01 us  [per_device(): lax.all_to_all(send_rows, 'fsdp', split_axis=0, concat_axis=0, tiled=True)]
    ppermute x4 -> x6, waiting for transfers between devices: 17.5 us -> 54.7 us  [gather_near(): return (lax.ppermute(own, 'tp', UP), lax.ppermute(own, 'tp', DOWN))]
    ppermute x2 -> x3, waiting for transfers between devices: 12.1 us -> 35.5 us  [gather_end(): return lax.ppermute(far2, 'tp', TO_ENDS)]
    ppermute x2, starting transfers between devices: 5.1 us -> 23.7 us  [scatter_end(): return lax.ppermute(parts[3], 'tp', FROM_ENDS)]
    all_gather x1, waiting for transfers between devices: 10.5 us -> 0.01 us  [per_device(): w_o = lax.all_gather(w_o_t, 'fsdp', axis=0, tiled=True)]
    ppermute x2, waiting for transfers between devices: 23.4 us -> 13.7 us  [scatter_far(): lax.ppermute(total2, 'tp', UP_IN)]
    unnamed x150 -> x128, local copies, waits for them, and re-layouts: 21.8 us -> 13.3 us
    ppermute x2 -> x3, waiting for transfers between devices: 29.7 us -> 36.5 us  [gather_far(): down2 = lax.ppermute(step1[1], 'tp', DOWN_MID)]
  transfers between devices with their start and end apart: 26 -> 31, of which waited for: 16 -> 15; matrix products, arithmetic and copies ran while one was open for 14% -> 13% of each run, Pallas kernels for 3% -> 2%
where the time goes in v1:
time: 380 us; the launch traced here: 376 us
  waiting for transfers between devices  169 us (44%)
  starting transfers between devices  89.4 us (24%)
  local copies, waits for them, and re-layouts  37.1 us (10%)
  Pallas kernels  31.4 us (8%)
  other arithmetic  21 us (6%)
  between operations  15.1 us (4%)
  matrix products  12.8 us (3%)
    ppermute x6, waiting for transfers between devices, gather_near(): return (lax.ppermute(own, 'tp', UP), lax.ppermute(own, 'tp', DOWN))  54.7 us
    ppermute x3, waiting for transfers between devices, gather_far(): down2 = lax.ppermute(step1[1], 'tp', DOWN_MID)  36.5 us
    ppermute x3, waiting for transfers between devices, gather_end(): return lax.ppermute(far2, 'tp', TO_ENDS)  35.5 us
    ppermute x2, starting transfers between devices, scatter_end(): return lax.ppermute(parts[3], 'tp', FROM_ENDS)  23.7 us
    ppermute x6, starting transfers between devices, gather_near(): return (lax.ppermute(own, 'tp', UP), lax.ppermute(own, 'tp', DOWN))  19 us
    ppermute x2, waiting for transfers between devices, scatter_near(): up3 = lax.ppermute(go_up.astype(jnp.bfloat16), 'tp', UP)  16.7 us
    pallas_call x2, Pallas kernels, attention(): pl.pallas_call(functools.partial(attention_kernel, bool(prev), is_last, f...  14.5 us
    ppermute x2, starting transfers between devices, scatter_near(): up3 = lax.ppermute(go_up.astype(jnp.bfloat16), 'tp', UP)  14.2 us
  transfers between devices with their start and end apart: 31, of which 15 were waited for; matrix products, arithmetic and copies ran while one was open for 13% of the time, Pallas kernels for 2%

profile of v1, /device:TPU:0, one launch (start us, length us, event | category | flops | bytes accessed | tf_op | source)
XLA Modules:
  0.0 375.6 jit_solution(6589230252366666934)
XLA Ops:
  12.1 5.2 %all-to-all-start = ((bf16[8,4,2]{1,2,0:T(2,128)(2,1)}), bf16[8,4,2]{1,2,0:T(2,128)(2,1)S(1)}, u32[]{:S(2)}, u32[]{:S(2)}) async-start(bf16[8,4,2]{1,2,0:T(2,128)(2,1)} %copy.47), calls=%async_computation | async-start | bytes 8192 | tf_op jit(solution)/shard_map/all_to_all | solution.py:375
  17.4 5.4 %gather_fusion = bf16[32,72,896]{2,1,0:T(8,128)(2,1)} fusion(bf16[32,72,896]{2,1,0:T(8,128)(2,1)} %param.10, s32[1024]{0:T(1024)S(1)} %pad_clamp_fusion.1), kind=kCustom, calls=%fused_computation | custom fusion | bytes 8257664 | tf_op jit(solution)/shard_map/jit(_take)/gather | solution.py:366
  34.3 18.0 %collective-permute-done = bf16[256,896]{1,0:T(8,128)(2,1)S(1)} collective-permute-done((bf16[256,896]{1,0:T(8,128)(2,1)S(1)}, bf16[256,896]{1,0:T(8,128)(2,1)S(1)}, u32[]{:S(2)}, u32[]{:S(2)}) %collective-permute-start) | collective-permute-done | bytes 458784 | tf_op jit(solution)/shard_map/ppermute | solution.py:45
  53.1 13.6 %collective-permute-done.2 = bf16[256,896]{1,0:T(8,128)(2,1)S(1)} collective-permute-done((bf16[256,896]{1,0:T(8,128)(2,1)S(1)}, bf16[256,896]{1,0:T(8,128)(2,1)S(1)}, u32[]{:S(2)}, u32[]{:S(2)}) %collective-permute-start.2) | collective-permute-done | bytes 458784 | tf_op jit(solution)/shard_map/ppermute | solution.py:45
  71.3 28.0 %collective-permute-done.3 = bf16[256,896]{1,0:T(8,128)(2,1)S(1)} collective-permute-done((bf16[256,896]{1,0:T(8,128)(2,1)S(1)}, bf16[256,896]{1,0:T(8,128)(2,1)S(1)}, u32[]{:S(2)}, u32[]{:S(2)}) %collective-permute-start.3) | collective-permute-done | bytes 458784 | tf_op jit(solution)/shard_map/ppermute | solution.py:50
  100.7 6.2 %gather_fusion.1 = bf16[768,896]{1,0:T(8,128)(2,1)S(1)} fusion(bf16[2304,896]{1,0:T(8,128)(2,1)} %bitcast.5, s32[1024]{0:T(1024)S(1)} %pad_clamp_fusion), kind=kCustom, calls=%fused_computation.1 | custom fusion | bytes 2755584 | tf_op jit(solution)/shard_map/jit(_take)/gather | solution.py:400
  107.0 5.8 %collective-permute-start.4 = (bf16[256,896]{1,0:T(8,128)(2,1)S(1)}, bf16[256,896]{1,0:T(8,128)(2,1)S(1)}, u32[]{:S(2)}, u32[]{:S(2)}) collective-permute-start(bf16[256,896]{1,0:T(8,128)(2,1)S(1)} %slice.105.refs_0_.refs_4_), channel_id=1, source_target_pairs={{0,1},{1,2},{2,3},{4,5},{5,6},{6,7},{8,9},{9,10},{10,11},{12,13},{... | collective-permute-start | bytes 1376264 | tf_op jit(solution)/shard_map/ppermute | solution.py:45
  115.1 7.5 %collective-permute-done.4 = bf16[256,896]{1,0:T(8,128)(2,1)S(1)} collective-permute-done((bf16[256,896]{1,0:T(8,128)(2,1)S(1)}, bf16[256,896]{1,0:T(8,128)(2,1)S(1)}, u32[]{:S(2)}, u32[]{:S(2)}) %collective-permute-start.4) | collective-permute-done | bytes 458784 | tf_op jit(solution)/shard_map/ppermute | solution.py:45
  123.9 5.9 %collective-permute-start.7 = (bf16[512,896]{1,0:T(8,128)(2,1)S(1)}, bf16[512,896]{1,0:T(8,128)(2,1)}, u32[]{:S(2)}, u32[]{:S(2)}) collective-permute-start(bf16[512,896]{1,0:T(8,128)(2,1)S(1)} %slice.104.refs_0_), channel_id=1, source_target_pairs={{0,1},{1,2},{2,3},{4,5},{5,6},{6,7},{8,9},{9,10},{10,11},{12,13},{... | collective-permute-start | bytes 2752520 | tf_op jit(solution)/shard_map/ppermute | solution.py:45
  132.7 15.6 %collective-permute-done.6 = bf16[512,896]{1,0:T(8,128)(2,1)S(1)} collective-permute-done((bf16[512,896]{1,0:T(8,128)(2,1)S(1)}, bf16[512,896]{1,0:T(8,128)(2,1)S(1)}, u32[]{:S(2)}, u32[]{:S(2)}) %collective-permute-start.6) | collective-permute-done | bytes 917536 | tf_op jit(solution)/shard_map/ppermute | solution.py:45
  149.6 8.5 %collective-permute-done.10 = bf16[256,896]{1,0:T(8,128)(2,1)S(1)} collective-permute-done((bf16[256,896]{1,0:T(8,128)(2,1)}, bf16[256,896]{1,0:T(8,128)(2,1)S(1)}, u32[]{:S(2)}, u32[]{:S(2)}) %collective-permute-start.10) | collective-permute-done | bytes 458784 | tf_op jit(solution)/shard_map/ppermute | solution.py:50
  168.3 17.8 %collective-permute-done.13 = bf16[256,896]{1,0:T(8,128)(2,1)S(1)} collective-permute-done((bf16[256,896]{1,0:T(8,128)(2,1)S(1)}, bf16[256,896]{1,0:T(8,128)(2,1)S(1)}, u32[]{:S(2)}, u32[]{:S(2)}) %collective-permute-start.13) | collective-permute-done | bytes 458784 | tf_op jit(solution)/shard_map/ppermute | solution.py:55
  215.4 16.9 %collective-permute-done.14 = bf16[512,896]{1,0:T(8,128)(2,1)S(1)} collective-permute-done((bf16[512,896]{1,0:T(8,128)(2,1)S(1)}, bf16[512,896]{1,0:T(8,128)(2,1)S(1)}, u32[]{:S(2)}, u32[]{:S(2)}) %collective-permute-start.14) | collective-permute-done | bytes 917536 | tf_op jit(solution)/shard_map/ppermute | solution.py:55
  234.2 8.8 %attention.2 = (bf16[384,768]{1,0:T(8,128)(2,1)S(1)}, bf16[384,768]{1,0:T(8,128)(2,1)S(1)}, f32[384,2]{1,0:T(8,128)S(1)}, bf16[512,512]{1,0:T(8,128)(2,1)S(1)}, ...) custom-call(f32[512,768]{1,0:T(8,128)S(1)} %get-tuple-element.46.ref, ...), custom_call_target="tpu_custom_call" | custom-call | flops 805306368 | bytes 4718592 | tf_op jit(solution)/shard_map/attention/pallas_call | solution.py:233
  244.1 12.7 %collective-permute-start.15 = (bf16[384,896]{1,0:T(8,128)(2,1)S(1)}, bf16[384,896]{1,0:T(8,128)(2,1)S(1)}, u32[]{:S(2)}, u32[]{:S(2)}) collective-permute-start(bf16[384,896]{1,0:T(8,128)(2,1)S(1)} %subtract_convert_fusion.5), channel_id=1, source_target_pairs={{3,2},{0,1},{7,6},{4,5},{11,10},{8,9},{15,14},{12,13},{19,18},{16,... | collective-permute-start | bytes 2064392 | tf_op jit(solution)/shard_map/ppermute | solution.py:70
  257.8 5.6 %attention.3 = (bf16[384,768]{1,0:T(8,128)(2,1)S(1)}, bf16[384,768]{1,0:T(8,128)(2,1)S(1)}, f32[384,2]{1,0:T(8,128)S(1)}, bf16[256,512]{1,0:T(8,128)(2,1)S(1)}) custom-call(f32[256,768]{1,0:T(8,128)S(1)} %get-tuple-element.51.refs_0_, f32[256,1]{1,0:T(8,128)S(1)} %get-tuple-element.52.refs_1_, f32[256,512]{1,0:T(8,128)S(1)} %fusion.5.refs_2_, ...), custom_call_target="tpu_custom_call" | custom-call | flops 402653184 | bytes 2359296 | tf_op jit(solution)/shard_map/attention/pallas_call | solution.py:233
  266.5 11.3 %weight_grads.1 = bf16[3584,1280]{1,0:T(8,128)(2,1)} custom-call(s32[4]{0:T(128)S(1)} %pad_add_fusion.place_ref, bf16[512,896]{1,0:T(8,128)(2,1)S(1)} %copy-done.33, bf16[512,896]{1,0:T(8,128)(2,1)S(1)} %copy-done.27, bf16[512,896]{1,0:T(8,128)(2,1)S(1)} %copy-done.30, bf16[512,896]{1,0:T(8,128)(2,1)S(1)} %select_select_fusion.refs_0_.refs_3_, ...), custom_call_target="tpu_custom_call" | custom-call | flops 7046430720 | bytes 20185088 | tf_op jit(solution)/shard_map/weight_grads/pallas_call | solution.py:317
  282.1 11.1 %collective-permute-start.20 = (bf16[384,896]{1,0:T(8,128)(2,1)S(1)}, bf16[384,896]{1,0:T(8,128)(2,1)S(1)}, u32[]{:S(2)}, u32[]{:S(2)}) collective-permute-start(bf16[384,896]{1,0:T(8,128)(2,1)S(1)} %subtract_convert_fusion.2), channel_id=1, source_target_pairs={{3,2},{0,1},{7,6},{4,5},{11,10},{8,9},{15,14},{12,13},{19,18},{16,... | collective-permute-start | bytes 2064392 | tf_op jit(solution)/shard_map/ppermute | solution.py:70
  297.5 9.8 %collective-permute-start.17 = (bf16[384,896]{1,0:T(8,128)(2,1)S(1)}, bf16[384,896]{1,0:T(8,128)(2,1)S(1)}, u32[]{:S(2)}, u32[]{:S(2)}) collective-permute-start(bf16[384,896]{1,0:T(8,128)(2,1)S(1)} %get-tuple-element.81), channel_id=1, source_target_pairs={{0,1},{1,2},{2,3},{4,5},{5,6},{6,7},{8,9},{9,10},{10,11},{12,13},{... | collective-permute-start | bytes 2064392 | tf_op jit(solution)/shard_map/ppermute | solution.py:87
  311.4 4.7 %collective-permute-start.21 = (bf16[384,896]{1,0:T(8,128)(2,1)S(1)}, bf16[384,896]{1,0:T(8,128)(2,1)S(1)}, u32[]{:S(2)}, u32[]{:S(2)}) collective-permute-start(bf16[384,896]{1,0:T(8,128)(2,1)S(1)} %add_convert_fusion.2), channel_id=1, source_target_pairs={{0,1},{1,2},{4,5},{5,6},{8,9},{9,10},{12,13},{13,14},{16,17},{17,1... | collective-permute-start | bytes 2064392 | tf_op jit(solution)/shard_map/ppermute | solution.py:78
  318.7 7.1 %collective-permute-done.17 = bf16[384,896]{1,0:T(8,128)(2,1)S(1)} collective-permute-done((bf16[384,896]{1,0:T(8,128)(2,1)S(1)}, bf16[384,896]{1,0:T(8,128)(2,1)S(1)}, u32[]{:S(2)}, u32[]{:S(2)}) %collective-permute-start.17) | collective-permute-done | bytes 688160 | tf_op jit(solution)/shard_map/ppermute | solution.py:87
  326.0 11.3 %collective-permute-done.21 = bf16[384,896]{1,0:T(8,128)(2,1)S(1)} collective-permute-done((bf16[384,896]{1,0:T(8,128)(2,1)S(1)}, bf16[384,896]{1,0:T(8,128)(2,1)S(1)}, u32[]{:S(2)}, u32[]{:S(2)}) %collective-permute-start.21) | collective-permute-done | bytes 688160 | tf_op jit(solution)/shard_map/ppermute | solution.py:78
  344.3 9.6 %collective-permute-done.22 = bf16[384,896]{1,0:T(8,128)(2,1)S(1)} collective-permute-done((bf16[384,896]{1,0:T(8,128)(2,1)S(1)}, bf16[384,896]{1,0:T(8,128)(2,1)S(1)}, u32[]{:S(2)}, u32[]{:S(2)}) %collective-permute-start.22) | collective-permute-done | bytes 688160 | tf_op jit(solution)/shard_map/ppermute | solution.py:87
  353.9 9.3 %collective-permute-done.24 = bf16[384,896]{1,0:T(8,128)(2,1)S(1)} collective-permute-done((bf16[384,896]{1,0:T(8,128)(2,1)S(1)}, bf16[384,896]{1,0:T(8,128)(2,1)S(1)}, u32[]{:S(2)}, u32[]{:S(2)}) %collective-permute-start.24) | collective-permute-done | bytes 688160 | tf_op jit(solution)/shard_map/ppermute | solution.py:88
  (262 shorter events, 104.9 us)
Async XLA Ops:
  7.2 124.0 %all-gather.4.cloned.1.call-start = ((), (), s32[]{:S(2)}) async-start(), calls=%async_computation.3 | async-start | bytes 4587520 | tf_op jit(solution)/shard_map/all_gather | solution.py:353
  9.5 180.9 %all-gather.6.cloned.1.call-start = ((), (), s32[]{:S(2)}) async-start(), calls=%async_computation.4 | async-start | bytes 6193152 | tf_op jit(solution)/shard_map/all_gather | solution.py:414
  22.7 78.0 %all-to-all-start.1 = ((bf16[32,72,896]{2,1,0:T(8,128)(2,1)}), bf16[32,72,896]{2,1,0:T(8,128)(2,1)}, u32[]{:S(2)}, u32[]{:S(2)}) async-start(bf16[32,72,896]{2,1,0:T(8,128)(2,1)} %gather_fusion), calls=%async_computation.1 | async-start | bytes 8257536 | tf_op jit(solution)/shard_map/all_to_all | solution.py:367
  27.3 174.5 %all-gather.8.cloned.1.call-start = ((), (), s32[]{:S(2)}) async-start(), calls=%async_computation.5 | async-start | bytes 4128768 | tf_op jit(solution)/shard_map/all_gather | solution.py:417
  28.4 23.9 %collective-permute-start = (bf16[256,896]{1,0:T(8,128)(2,1)S(1)}, bf16[256,896]{1,0:T(8,128)(2,1)S(1)}, u32[]{:S(2)}, u32[]{:S(2)}) collective-permute-start(bf16[256,896]{1,0:T(8,128)(2,1)S(1)} %slice.81.refs_8_), channel_id=1, source_target_pairs={{0,1},{1,2},{2,3},{4,5},{5,6},{6,7},{8,9},{9,10},{10,11},{12,13},{... | collective-permute-start | bytes 1376264 | tf_op jit(solution)/shard_map/ppermute | solution.py:45
  31.9 34.8 %collective-permute-start.2 = (bf16[256,896]{1,0:T(8,128)(2,1)S(1)}, bf16[256,896]{1,0:T(8,128)(2,1)S(1)}, u32[]{:S(2)}, u32[]{:S(2)}) collective-permute-start(bf16[256,896]{1,0:T(8,128)(2,1)S(1)} %slice.81.refs_8_), channel_id=1, source_target_pairs={{1,0},{2,1},{3,2},{5,4},{6,5},{7,6},{9,8},{10,9},{11,10},{13,12},{... | collective-permute-start | bytes 1376264 | tf_op jit(solution)/shard_map/ppermute | solution.py:45
  33.2 331.8 %reduce-scatter.2.cloned.1.call-start = ((), (), s32[]{:S(2)}) async-start(), calls=%async_computation.6 | async-start | bytes 10321920 | tf_op jit(solution)/shard_map/reduce_scatter | solution.py:476
  52.4 18.9 %collective-permute-start.1 = (bf16[256,896]{1,0:T(8,128)(2,1)S(1)}, bf16[256,896]{1,0:T(8,128)(2,1)S(1)}, u32[]{:S(2)}, u32[]{:S(2)}) collective-permute-start(bf16[256,896]{1,0:T(8,128)(2,1)S(1)} %collective-permute-done), channel_id=1, source_target_pairs={{1,2},{2,3},{5,6},{6,7},{9,10},{10,11},{13,14},{14,15},{17,18},{18... | collective-permute-start | bytes 1376264 | tf_op jit(solution)/shard_map/ppermute | solution.py:49
  66.7 32.7 %collective-permute-start.3 = (bf16[256,896]{1,0:T(8,128)(2,1)S(1)}, bf16[256,896]{1,0:T(8,128)(2,1)S(1)}, u32[]{:S(2)}, u32[]{:S(2)}) collective-permute-start(bf16[256,896]{1,0:T(8,128)(2,1)S(1)} %collective-permute-done.2), channel_id=1, source_target_pairs={{1,0},{2,1},{5,4},{6,5},{9,8},{10,9},{13,12},{14,13},{17,16},{18,1... | collective-permute-start | bytes 1376264 | tf_op jit(solution)/shard_map/ppermute | solution.py:50
  122.6 25.6 %collective-permute-start.6 = (bf16[512,896]{1,0:T(8,128)(2,1)S(1)}, bf16[512,896]{1,0:T(8,128)(2,1)S(1)}, u32[]{:S(2)}, u32[]{:S(2)}) collective-permute-start(bf16[512,896]{1,0:T(8,128)(2,1)S(1)} %slice.104.refs_0_), channel_id=1, source_target_pairs={{1,0},{2,1},{3,2},{5,4},{6,5},{7,6},{9,8},{10,9},{11,10},{13,12},{... | collective-permute-start | bytes 2752520 | tf_op jit(solution)/shard_map/ppermute | solution.py:45
  123.9 36.1 %collective-permute-start.7 = (bf16[512,896]{1,0:T(8,128)(2,1)S(1)}, bf16[512,896]{1,0:T(8,128)(2,1)}, u32[]{:S(2)}, u32[]{:S(2)}) collective-permute-start(bf16[512,896]{1,0:T(8,128)(2,1)S(1)} %slice.104.refs_0_), channel_id=1, source_target_pairs={{0,1},{1,2},{2,3},{4,5},{5,6},{6,7},{8,9},{9,10},{10,11},{12,13},{... | collective-permute-start | bytes 2752520 | tf_op jit(solution)/shard_map/ppermute | solution.py:45
  129.9 28.2 %collective-permute-start.10 = (bf16[256,896]{1,0:T(8,128)(2,1)}, bf16[256,896]{1,0:T(8,128)(2,1)S(1)}, u32[]{:S(2)}, u32[]{:S(2)}) collective-permute-start(bf16[256,896]{1,0:T(8,128)(2,1)} %collective-permute-done.9), channel_id=1, source_target_pairs={{1,0},{2,1},{5,4},{6,5},{9,8},{10,9},{13,12},{14,13},{17,16},{18,1... | collective-permute-start | bytes 1376264 | tf_op jit(solution)/shard_map/ppermute | solution.py:50
  131.2 27.7 %collective-permute-start.8 = (bf16[256,896]{1,0:T(8,128)(2,1)}, bf16[256,896]{1,0:T(8,128)(2,1)}, u32[]{:S(2)}, u32[]{:S(2)}) collective-permute-start(bf16[256,896]{1,0:T(8,128)(2,1)} %copy-done.52), channel_id=1, source_target_pairs={{1,2},{2,3},{5,6},{6,7},{9,10},{10,11},{13,14},{14,15},{17,18},{18... | collective-permute-start | bytes 1376264 | tf_op jit(solution)/shard_map/ppermute | solution.py:49
  148.3 39.9 %collective-permute-start.12 = (bf16[512,896]{1,0:T(8,128)(2,1)S(1)}, bf16[512,896]{1,0:T(8,128)(2,1)}, u32[]{:S(2)}, u32[]{:S(2)}) collective-permute-start(bf16[512,896]{1,0:T(8,128)(2,1)S(1)} %collective-permute-done.6), channel_id=1, source_target_pairs={{1,0},{2,1},{5,4},{6,5},{9,8},{10,9},{13,12},{14,13},{17,16},{18,1... | collective-permute-start | bytes 2752520 | tf_op jit(solution)/shard_map/ppermute | solution.py:50
  160.0 28.1 %collective-permute-start.11 = (bf16[512,896]{1,0:T(8,128)(2,1)}, bf16[512,896]{1,0:T(8,128)(2,1)}, u32[]{:S(2)}, u32[]{:S(2)}) collective-permute-start(bf16[512,896]{1,0:T(8,128)(2,1)} %collective-permute-done.7), channel_id=1, source_target_pairs={{1,2},{2,3},{5,6},{6,7},{9,10},{10,11},{13,14},{14,15},{17,18},{18... | collective-permute-start | bytes 2752520 | tf_op jit(solution)/shard_map/ppermute | solution.py:49
  163.6 22.4 %collective-permute-start.13 = (bf16[256,896]{1,0:T(8,128)(2,1)S(1)}, bf16[256,896]{1,0:T(8,128)(2,1)S(1)}, u32[]{:S(2)}, u32[]{:S(2)}) collective-permute-start(bf16[256,896]{1,0:T(8,128)(2,1)S(1)} %broadcast_select_fusion.4.refs_2_.refs_6_), channel_id=1, source_target_pairs={{2,3},{1,0},{6,7},{5,4},{10,11},{9,8},{14,15},{13,12},{18,19},{17,... | collective-permute-start | bytes 1376264 | tf_op jit(solution)/shard_map/ppermute | solution.py:55
  209.4 22.9 %collective-permute-start.14 = (bf16[512,896]{1,0:T(8,128)(2,1)S(1)}, bf16[512,896]{1,0:T(8,128)(2,1)S(1)}, u32[]{:S(2)}, u32[]{:S(2)}) collective-permute-start(bf16[512,896]{1,0:T(8,128)(2,1)S(1)} %copy-done.30), channel_id=1, source_target_pairs={{2,3},{1,0},{6,7},{5,4},{10,11},{9,8},{14,15},{13,12},{18,19},{17,... | collective-permute-start | bytes 2752520 | tf_op jit(solution)/shard_map/ppermute | solution.py:55
  244.1 20.1 %collective-permute-start.15 = (bf16[384,896]{1,0:T(8,128)(2,1)S(1)}, bf16[384,896]{1,0:T(8,128)(2,1)S(1)}, u32[]{:S(2)}, u32[]{:S(2)}) collective-permute-start(bf16[384,896]{1,0:T(8,128)(2,1)S(1)} %subtract_convert_fusion.5), channel_id=1, source_target_pairs={{3,2},{0,1},{7,6},{4,5},{11,10},{8,9},{15,14},{12,13},{19,18},{16,... | collective-permute-start | bytes 2064392 | tf_op jit(solution)/shard_map/ppermute | solution.py:70
  282.1 28.9 %collective-permute-start.20 = (bf16[384,896]{1,0:T(8,128)(2,1)S(1)}, bf16[384,896]{1,0:T(8,128)(2,1)S(1)}, u32[]{:S(2)}, u32[]{:S(2)}) collective-permute-start(bf16[384,896]{1,0:T(8,128)(2,1)S(1)} %subtract_convert_fusion.2), channel_id=1, source_target_pairs={{3,2},{0,1},{7,6},{4,5},{11,10},{8,9},{15,14},{12,13},{19,18},{16,... | collective-permute-start | bytes 2064392 | tf_op jit(solution)/shard_map/ppermute | solution.py:70
  297.5 28.3 %collective-permute-start.17 = (bf16[384,896]{1,0:T(8,128)(2,1)S(1)}, bf16[384,896]{1,0:T(8,128)(2,1)S(1)}, u32[]{:S(2)}, u32[]{:S(2)}) collective-permute-start(bf16[384,896]{1,0:T(8,128)(2,1)S(1)} %get-tuple-element.81), channel_id=1, source_target_pairs={{0,1},{1,2},{2,3},{4,5},{5,6},{6,7},{8,9},{9,10},{10,11},{12,13},{... | collective-permute-start | bytes 2064392 | tf_op jit(solution)/shard_map/ppermute | solution.py:87
  307.3 18.5 %collective-permute-start.19 = (bf16[384,896]{1,0:T(8,128)(2,1)S(1)}, bf16[384,896]{1,0:T(8,128)(2,1)S(1)}, u32[]{:S(2)}, u32[]{:S(2)}) collective-permute-start(bf16[384,896]{1,0:T(8,128)(2,1)S(1)} %get-tuple-element.82), channel_id=1, source_target_pairs={{1,0},{2,1},{3,2},{5,4},{6,5},{7,6},{9,8},{10,9},{11,10},{13,12},{... | collective-permute-start | bytes 2064392 | tf_op jit(solution)/shard_map/ppermute | solution.py:88
  311.4 25.9 %collective-permute-start.21 = (bf16[384,896]{1,0:T(8,128)(2,1)S(1)}, bf16[384,896]{1,0:T(8,128)(2,1)S(1)}, u32[]{:S(2)}, u32[]{:S(2)}) collective-permute-start(bf16[384,896]{1,0:T(8,128)(2,1)S(1)} %add_convert_fusion.2), channel_id=1, source_target_pairs={{0,1},{1,2},{4,5},{5,6},{8,9},{9,10},{12,13},{13,14},{16,17},{17,1... | collective-permute-start | bytes 2064392 | tf_op jit(solution)/shard_map/ppermute | solution.py:78
  316.1 21.2 %collective-permute-start.23 = (bf16[384,896]{1,0:T(8,128)(2,1)S(1)}, bf16[384,896]{1,0:T(8,128)(2,1)S(1)}, u32[]{:S(2)}, u32[]{:S(2)}) collective-permute-start(bf16[384,896]{1,0:T(8,128)(2,1)S(1)} %add_convert_fusion.2), channel_id=1, source_target_pairs={{3,2},{2,1},{7,6},{6,5},{11,10},{10,9},{15,14},{14,13},{19,18},{18... | collective-permute-start | bytes 2064392 | tf_op jit(solution)/shard_map/ppermute | solution.py:78
  342.1 21.1 %collective-permute-start.24 = (bf16[384,896]{1,0:T(8,128)(2,1)S(1)}, bf16[384,896]{1,0:T(8,128)(2,1)S(1)}, u32[]{:S(2)}, u32[]{:S(2)}) collective-permute-start(bf16[384,896]{1,0:T(8,128)(2,1)S(1)} %get-tuple-element.80), channel_id=1, source_target_pairs={{1,0},{2,1},{3,2},{5,4},{6,5},{7,6},{9,8},{10,9},{11,10},{13,12},{... | collective-permute-start | bytes 2064392 | tf_op jit(solution)/shard_map/ppermute | solution.py:88
  (73 other events, 730.2 us)
Sparse Core Ops, SparseCore 0:
  10.2 94.1 all-gather.3
  106.2 40.7 all-gather.5
  148.9 34.5 all-gather.7
  277.9 80.0 reduce-scatter.1
